TPU v7x, 1024 devices: a whole 8x8x8 slice. The times are simulated.
1024 devices in a mesh: ctx: 64 (over z, x), dp: 4 (over y_lo), section: 4 (over y_hi, core).
Axes of the slice: x: 8, y: 8 (y_hi: 2, y_lo: 4; y = y_hi * 4 + y_lo), z: 8, core: 2. Of those that a mesh axis runs over, the one named last changes fastest.
Arguments:
- tokens: bfloat16 [4, 4, 8192, 4096], P('section', 'dp', 'ctx'), may hold values from -6 to 6
- norm_gain: float32 [4, 4096], P('section'), may hold values from 0.1 to 1.9
- query_weight: bfloat16 [4, 4096, 512], P('section', 'dp'), may hold values from -0.421875 to 0.421875
- key_weight: bfloat16 [4, 4096, 128], P('section', 'dp'), may hold values from -0.421875 to 0.421875
- value_weight: bfloat16 [4, 4096, 128], P('section', 'dp'), may hold values from -0.09375 to 0.09375
- block_order: int32 [4, 4, 128], P('section', 'dp'), may hold values from 0 to 127, each once within a row
- doc_ids: int32 [4, 4, 8192], P('section', 'dp'), may hold values from 0 to 3, never falling along the last dimension, each value on 1 to 4096 neighbouring positions
Outputs:
- passed: bfloat16 [4, 4, 8192, 512], P('section', 'dp', 'ctx')
Inputs may be any that keep to these rules, and one draw needn't show every extreme that they name: `block_order`: each row is a permutation of the block numbers. `doc_ids`: never falling along positions; every document holds 1 to 4096 positions, and one holds exactly 4096.
All inputs are finite; a program needn't handle non-finite values.
Results may differ from a plain program's by a relative error of at most 0.012.
Values may be sent and summed in bfloat16 or wider, within the bound.
A program may use at most 32 MiB of HBM per device.

v0:
```python
import jax
import jax.numpy as jnp
from jax import lax
from jax.sharding import PartitionSpec as P

ROPE_BASE = 500000.0
EPSILON = 1e-05
MASKED = -1e30


def passed_along(x, axis, by):
    length = lax.axis_size(axis)
    return lax.ppermute(x, axis, [(i, (i + by) % length) for i in range(length)])


def rotate_pairs(values, positions, head_size):
    count_rows = values.shape[0]
    shaped = values.reshape(count_rows, -1, head_size)
    halfway = head_size // 2
    freqs = ROPE_BASE ** (-jnp.arange(halfway, dtype=jnp.float32) * 2.0 / head_size)
    angles = positions.astype(jnp.float32)[:, None, None] * freqs[None, None, :]
    cosine = jnp.cos(angles)
    sine = jnp.sin(angles)
    first_half = shaped[..., :halfway]
    second_half = shaped[..., halfway:]
    turned = jnp.concatenate(
        [first_half * cosine - second_half * sine, second_half * cosine + first_half * sine],
        axis=-1,
    )
    return turned.reshape(count_rows, -1)


def local(tokens, norm_gain, query_weight, key_weight, value_weight, block_order, doc_ids):
    rows_here = tokens[0, 0]
    row_count = rows_here.shape[0]
    block_rows = doc_ids.shape[2] // block_order.shape[2]
    head_size = key_weight.shape[2]
    query_width = query_weight.shape[2]
    query_heads = query_width // head_size
    widened = rows_here.astype(jnp.float32)
    normed = (
        widened
        * lax.rsqrt(jnp.mean(widened * widened, axis=-1, keepdims=True) + EPSILON)
        * norm_gain[0][None, :]
    ).astype(jnp.bfloat16)
    pieces = (
        lax.all_gather(query_weight, "dp", axis=1, tiled=True),
        lax.all_gather(key_weight, "dp", axis=1, tiled=True),
        lax.all_gather(value_weight, "dp", axis=1, tiled=True),
    )
    q_raw, k_raw, v_raw = tuple(
        (jnp.dot(normed, piece[0], preferred_element_type=jnp.float32) for piece in pieces)
    )
    order = block_order[0, 0]
    within = jnp.arange(block_rows, dtype=jnp.int32)
    all_positions = (order[:, None] * block_rows + within[None, :]).reshape(-1)
    key_documents = jnp.take(doc_ids[0, 0], all_positions)
    cycle_index = lax.axis_index("ctx")
    query_positions = lax.dynamic_slice_in_dim(all_positions, cycle_index * row_count, row_count)
    query_documents = lax.dynamic_slice_in_dim(key_documents, cycle_index * row_count, row_count)
    queries = (
        rotate_pairs(q_raw, query_positions, head_size)
        .astype(jnp.bfloat16)
        .reshape(row_count, query_heads, head_size)
        .transpose(1, 0, 2)
    )
    keys = rotate_pairs(k_raw, query_positions, head_size).astype(jnp.bfloat16)
    values = v_raw.astype(jnp.bfloat16)
    scaling = head_size ** (-0.5)

    def absorb(state, key_block, value_block, key_pos, key_doc):
        run_max, run_total, run_acc = state
        scores = (
            jnp.einsum("hqd,kd->hqk", queries, key_block, preferred_element_type=jnp.float32)
            * scaling
        )
        allowed = (key_doc[None, :] == query_documents[:, None]) & (
            key_pos[None, :] <= query_positions[:, None]
        )
        scores = jnp.where(allowed[None], scores, MASKED)
        new_max = jnp.maximum(run_max, jnp.max(scores, axis=-1))
        weights = jnp.where(allowed[None], jnp.exp(scores - new_max[..., None]), 0.0)
        factor = jnp.exp(run_max - new_max)
        new_total = run_total * factor + jnp.sum(weights, axis=-1)
        new_acc = run_acc * factor[..., None] + jnp.einsum(
            "hqk,kd->hqd",
            weights.astype(jnp.bfloat16),
            value_block,
            preferred_element_type=jnp.float32,
        )
        return (new_max, new_total, new_acc)

    starting_state = (
        jnp.full((query_heads, row_count), MASKED, jnp.float32),
        jnp.zeros((query_heads, row_count), jnp.float32),
        jnp.zeros((query_heads, row_count, head_size), jnp.float32),
    )
    key_piece = lax.all_gather(keys, "ctx", axis=0, tiled=True)
    value_piece = lax.all_gather(values, "ctx", axis=0, tiled=True)
    piece_rows = key_piece.shape[0]
    key_pos = all_positions
    key_doc = key_documents
    groups = piece_rows // 1024

    def inner(inner_state, stacked):
        return (absorb(inner_state, stacked[0], stacked[1], stacked[2], stacked[3]), None)

    stacked_all = (
        key_piece.reshape(groups, 1024, -1),
        value_piece.reshape(groups, 1024, -1),
        key_pos.reshape(groups, 1024),
        key_doc.reshape(groups, 1024),
    )
    result, unused = lax.scan(inner, starting_state, stacked_all)
    final_max, final_total, final_acc = result
    attended = (
        (final_acc / final_total[..., None])
        .transpose(1, 0, 2)
        .reshape(row_count, query_width)
        .astype(jnp.bfloat16)
    )
    passed = passed_along(attended, "section", 1)
    return passed[None, None]


def solution(mesh):
    in_specs = (
        P("section", "dp", "ctx", None),
        P("section", None),
        P("section", "dp", None),
        P("section", "dp", None),
        P("section", "dp", None),
        P("section", "dp", None),
        P("section", "dp", None),
    )
    out_specs = P("section", "dp", "ctx", None)
    return jax.shard_map(local, mesh=mesh, in_specs=in_specs, out_specs=out_specs, check_vma=False)
```

profile of v0, /device:TPU:32, one launch (start us, length us, event | category | flops | bytes accessed | tf_op | source)
XLA Modules:
  0.0 429.0 jit_solution(7133895107619554229)
XLA Ops:
  6.5 0.7 all-gather.7.cloned.1.call-update
  7.3 0.7 all-gather.11.cloned.1.call-update
  8.1 0.7 multiply_reduce_fusion
  9.0 1.5 fusion.19
  10.5 47.9 %all-gather.7.cloned.1.call-done = bf16[1,4096,128]{2,1,0:T(8,128)(2,1)} async-done(((bf16[1,1024,128]{2,1,0:T(8,128)(2,1)}), bf16[1,4096,128]{2,1,0:T(8,128)(2,1)}) %all-gather.7.cloned.1.call-update) | async-done | bytes 1048592 | tf_op jit(solution)/shard_map/all_gather | solution.py:48
  58.4 2.2 convolution_bitcast_fusion
  60.6 0.2 fusion.34
  60.8 0.6 pad_maximum_fusion
  61.5 0.5 all-gather.9.cloned.1.call-update
  62.1 37.6 %all-gather.11.cloned.1.call-done = bf16[1,4096,128]{2,1,0:T(8,128)(2,1)} async-done(((bf16[1,1024,128]{2,1,0:T(8,128)(2,1)}), bf16[1,4096,128]{2,1,0:T(8,128)(2,1)}) %all-gather.11.cloned.1.call-update) | async-done | bytes 1048592 | tf_op jit(solution)/shard_map/all_gather | solution.py:49
  99.6 2.4 convolution_convert_fusion
  102.5 45.5 %gather_fusion = s32[8192]{0:T(1024)S(1)} fusion(s32[8192]{0:T(1024)S(1)} %bitcast.78, s32[8192]{0:T(1024)S(1)} %broadcast_clamp_fusion), kind=kCustom, calls=%fused_computation | custom fusion | bytes 98304 | tf_op jit(solution)/shard_map/jit(_take)/gather | solution.py:57
  148.2 0.2 multiply_cosine_fusion
  148.4 0.6 and_select_fusion
  149.0 46.3 %all-gather.15.cloned.1.call-done = bf16[8192,1,128]{0,2,1:T(8,128)(2,1)} async-done(((bf16[128,1,128]{0,2,1:T(8,128)(2,1)}), bf16[8192,1,128]{0,2,1:T(8,128)(2,1)}) %all-gather.15.cloned.1.call-update) | async-done | bytes 2097168 | tf_op jit(solution)/shard_map/all_gather | solution.py:98
  195.3 3.2 copy.19
  198.5 84.2 %all-gather.9.cloned.1.call-done = bf16[1,4096,512]{2,1,0:T(8,128)(2,1)} async-done(((bf16[1,1024,512]{2,1,0:T(8,128)(2,1)}), bf16[1,4096,512]{2,1,0:T(8,128)(2,1)}) %all-gather.9.cloned.1.call-update) | async-done | bytes 4194320 | tf_op jit(solution)/shard_map/all_gather | solution.py:47
  282.7 6.5 %copy.14 = bf16[512,4096]{1,0:T(8,128)(2,1)} copy(bf16[512,4096]{0,1:T(8,128)(2,1)} %bitcast.80) | data formatting | bytes 8388608 | tf_op jit(solution)/shard_map/dot_general | solution.py:52
  289.2 3.5 fusion.22
  292.9 85.6 %all-gather.13.cloned.1.call-done = bf16[8192,128]{1,0:T(8,128)(2,1)} async-done(((bf16[128,128]{1,0:T(8,128)(2,1)}), bf16[8192,128]{1,0:T(8,128)(2,1)}) %all-gather.13.cloned.1.call-update) | async-done | bytes 2097168 | tf_op jit(solution)/shard_map/all_gather | solution.py:99
  378.5 31.5 %while.15 = (s32[]{:T(128)}, f32[4,128]{1,0:T(4,128)S(1)}, f32[4,128]{1,0:T(4,128)S(1)}, f32[4,128,128]{2,1,0:T(8,128)S(1)}, s32[8,1024]{1,0:T(8,128)S(1)}, /*in...) while((s32[]{:T(128)}, f32[4,128]{1,0:T(4,128)S(1)}, ...), condition=%wide.region_4.5_spmd.clone, body=%wide.region_1.4_spmd.clone.sunk | while | flops 275843584 | bytes 8053917 | solution.py:114
  378.5 0.8 constant_dynamic-slice_fusion.3
  379.3 0.3 compare_and_fusion.2
  379.7 0.4 fusion.53
  380.1 0.5 fusion.54
  380.7 1.8 convolution_add_fusion.2
  382.5 0.8 constant_dynamic-slice_fusion.3
  383.3 0.3 compare_and_fusion.2
  383.6 0.4 fusion.53
  384.1 0.5 fusion.54
  384.6 1.8 convolution_add_fusion.2
  386.4 0.8 constant_dynamic-slice_fusion.3
  387.2 0.3 compare_and_fusion.2
  387.5 0.4 fusion.53
  388.0 0.5 fusion.54
  388.6 1.8 convolution_add_fusion.2
  390.4 0.8 constant_dynamic-slice_fusion.3
  391.1 0.3 compare_and_fusion.2
  391.5 0.4 fusion.53
  391.9 0.5 fusion.54
  392.5 1.8 convolution_add_fusion.2
  394.3 0.8 constant_dynamic-slice_fusion.3
  395.1 0.3 compare_and_fusion.2
  395.4 0.4 fusion.53
  395.9 0.5 fusion.54
  396.4 1.8 convolution_add_fusion.2
  398.2 0.8 constant_dynamic-slice_fusion.3
  399.0 0.3 compare_and_fusion.2
  399.4 0.4 fusion.53
  399.8 0.5 fusion.54
  400.4 1.8 convolution_add_fusion.2
  402.2 0.8 constant_dynamic-slice_fusion.3
  403.0 0.3 compare_and_fusion.2
  403.3 0.4 fusion.53
  403.8 0.5 fusion.54
  404.3 1.8 convolution_add_fusion.2
  406.1 0.8 constant_dynamic-slice_fusion.3
  406.9 0.3 compare_and_fusion.2
  407.2 0.4 fusion.53
  407.7 0.5 fusion.54
  408.3 1.8 convolution_add_fusion.2
  410.2 1.9 collective-permute-start
  412.1 9.7 %collective-permute-done = bf16[128,512]{1,0:T(8,128)(2,1)S(1)} collective-permute-done((bf16[128,512]{1,0:T(8,128)(2,1)S(1)}, bf16[128,512]{1,0:T(8,128)(2,1)S(1)}, u32[]{:S(2)}, u32[]{:S(2)}) %collective-permute-start) | collective-permute-done | bytes 131104 | tf_op jit(solution)/shard_map/ppermute | solution.py:13
  421.8 0.7 copy.35
  (61 shorter events, 1.5 us)
Async XLA Ops:
  6.5 96.0 %copy-start = (s32[1,1,8192]{2,1,0:T(1,128)S(1)}, s32[1,1,8192]{2,1,0:T(1,128)}, u32[]{:S(2)}) copy-start(s32[1,1,8192]{2,1,0:T(1,128)} %param.15) | copy-start | bytes 98308
  6.5 51.9 %all-gather.7.cloned.1.call-start = ((), (), s32[]{:S(2)}) async-start(), calls=%async_computation | async-start | bytes 1310720 | tf_op jit(solution)/shard_map/all_gather | solution.py:48
  7.3 92.4 %all-gather.11.cloned.1.call-start = ((), (), s32[]{:S(2)}) async-start(), calls=%async_computation.2 | async-start | bytes 1310720 | tf_op jit(solution)/shard_map/all_gather | solution.py:49
  8.0 187.3 %all-gather.15.cloned.1.call-start = ((), (), s32[]{:S(2)}) async-start(), calls=%async_computation.4 | async-start | bytes 2129920 | tf_op jit(solution)/shard_map/all_gather | solution.py:98
  10.5 89.1 %copy-start.1 = (bf16[1,1,128,4096]{3,2,1,0:T(8,128)(2,1)S(1)}, bf16[1,1,128,4096]{3,2,1,0:T(8,128)(2,1)}, u32[]{:S(2)}) copy-start(bf16[1,1,128,4096]{3,2,1,0:T(8,128)(2,1)} %param.9) | copy-start | bytes 3145732
  10.5 89.1 %copy-start.2 = (f32[1,4096]{1,0:T(1,128)S(1)}, f32[1,4096]{1,0:T(1,128)}, u32[]{:S(2)}) copy-start(f32[1,4096]{1,0:T(1,128)} %param.10) | copy-start | bytes 49156
  10.5 91.4 %copy-start.3 = (f32[128]{0:T(128)}, f32[128]{0:T(128)S(1)}, u32[]{:S(2)}) copy-start(f32[128]{0:T(128)S(1)} %add_rsqrt_fusion) | copy-start | bytes 1540
  61.4 221.2 %all-gather.9.cloned.1.call-start = ((), (), s32[]{:S(2)}) async-start(), calls=%async_computation.1 | async-start | bytes 5242880 | tf_op jit(solution)/shard_map/all_gather | solution.py:47
  62.0 316.5 %all-gather.13.cloned.1.call-start = ((), (), s32[]{:S(2)}) async-start(), calls=%async_computation.3 | async-start | bytes 2129920 | tf_op jit(solution)/shard_map/all_gather | solution.py:99
  410.2 11.6 %collective-permute-start = (bf16[128,512]{1,0:T(8,128)(2,1)S(1)}, bf16[128,512]{1,0:T(8,128)(2,1)S(1)}, u32[]{:S(2)}, u32[]{:S(2)}) collective-permute-start(bf16[128,512]{1,0:T(8,128)(2,1)S(1)} %copy_bitcast_fusion), channel_id=1, source_target_pairs={{0,1},{1,2},{2,3},{3,0},{4,5},{5,6},{6,7},{7,4},{8,9},{9,10},{10,1... | collective-permute-start | bytes 393224 | tf_op jit(solution)/shard_map/ppermute | solution.py:13
Sparse Core Ops, SparseCore 0:
  10.0 48.3 all-gather.6
  61.1 38.4 all-gather.10
  103.8 91.4 all-gather.14
  197.8 84.8 all-gather.8
  286.8 91.7 all-gather.12
where the time goes:
time: 430 us; the launch traced here: 429 us
  waiting for transfers between devices  313 us (73%)
  local copies, waits for them, and re-layouts  62.8 us (15%)
  matrix products  25.8 us (6%)
  between operations  13.3 us (3%)
  other arithmetic  11.5 us (3%)
    all_gather x1, waiting for transfers between devices, local(): value_piece = lax.all_gather(values, 'ctx', axis=0, tiled=True)  85.6 us
    all_gather x1, waiting for transfers between devices, local(): lax.all_gather(query_weight, 'dp', axis=1, tiled=True)  84.2 us
    all_gather x1, waiting for transfers between devices, local(): lax.all_gather(key_weight, 'dp', axis=1, tiled=True)  47.9 us
    all_gather x1, waiting for transfers between devices, local(): key_piece = lax.all_gather(keys, 'ctx', axis=0, tiled=True)  46.3 us
    gather x2, local copies, waits for them, and re-layouts, local(): key_documents = jnp.take(doc_ids[0, 0], all_positions)  45.5 us
    all_gather x1, waiting for transfers between devices, local(): lax.all_gather(value_weight, 'dp', axis=1, tiled=True)  37.6 us
    dot_general x8, matrix products, absorb(): jnp.einsum('hqk,kd->hqd', weights.astype(jnp.bfloat16), value_block, pref...  14.2 us
    ppermute x1, waiting for transfers between devices, passed_along(): lax.ppermute(x, axis, [(i, (i + by) % length) for i in range(length)])  9.68 us
  transfers between devices with their start and end apart: 6, of which 6 were waited for; matrix products, arithmetic and copies ran while one was open for 16% of the time, Pallas kernels for 0%

commit v1 on v0

v1 whole, which is shorter than its diff:
```python
import math

import jax
import jax.numpy as jnp
import numpy as np
from jax import lax
from jax.experimental import pallas as pl
from jax.experimental.pallas import tpu as pltpu
from jax.sharding import PartitionSpec as P

ROPE_BASE = 500000.0
EPSILON = 1e-05
FLOOR = -1e30
MASKED = -3e30
MESH = pl.DeviceIdType.MESH
F32 = jnp.float32
BF16 = jnp.bfloat16
RING = 8
HEAD = 128
BLOCK = 64


def rope_tables():
    freqs = ROPE_BASE ** (-np.arange(HEAD // 2, dtype=np.float64) * 2.0 / HEAD)
    coarse = np.arange(128, dtype=np.float64)[:, None] * BLOCK * freqs[None, :]
    fine = np.arange(BLOCK, dtype=np.float64)[:, None] * freqs[None, :]
    rows = [np.cos(coarse), np.sin(coarse), np.cos(fine), np.sin(fine)]
    table = np.concatenate(rows, axis=0)
    return np.concatenate([table, table], axis=1).astype(np.float32)


def wrap(i):
    return lax.rem(i + 2 * RING, RING)


class Gather:
    def __init__(self, bufs, rows, x, z, near_send, near_recv, far_send, far_recv):
        self.bufs, self.rows = bufs, rows
        self.small = (x, z)
        self.big = (z, x)
        self.near_send, self.near_recv = near_send, near_recv
        self.far_send, self.far_recv = far_send, far_recv
        self.x, self.z = x, z

    def small_device(self, half, by):
        if half == 0:
            return {"ctx": self.z * RING + wrap(self.x + by)}
        return {"ctx": wrap(self.z + by) * RING + self.x}

    def big_device(self, half, by):
        return self.small_device(1 - half, by)

    def slots(self, half, big, small, count):
        start = pl.multiple_of((big * RING + small) * self.rows, self.rows)
        return self.bufs[half].at[pl.ds(start, count * self.rows), :]

    def near(self, half, way, step, small):
        ref = self.slots(half, self.big[half], small, 1)
        return pltpu.make_async_remote_copy(
            src_ref=ref, dst_ref=ref,
            send_sem=self.near_send.at[half, way, step - 1],
            recv_sem=self.near_recv.at[half, way, step - 1],
            device_id=self.small_device(half, 1 - 2 * way), device_id_type=MESH)

    def far(self, half, way, hop, part, big, small, count):
        ref = self.slots(half, big, small, count)
        return pltpu.make_async_remote_copy(
            src_ref=ref, dst_ref=ref,
            send_sem=self.far_send.at[half, way, hop - 1, part],
            recv_sem=self.far_recv.at[half, way, hop - 1, part],
            device_id=self.big_device(half, 1 - 2 * way), device_id_type=MESH)

    def first_hop(self, half, small):
        for way in range(2):
            self.far(half, way, 1, small // 4, self.big[half], small, 1).start()

    def begin(self):
        for half in range(2):
            for way in range(2):
                self.near(half, way, 1, self.small[half]).start()
            self.first_hop(half, self.small[half])

    def near_steps(self):
        for step in range(1, 5):
            for half in range(2):
                for way in range(2):
                    if step == 4 and way == 1:
                        continue
                    came = wrap(self.small[half] - step * (1 - 2 * way))
                    self.near(half, way, step, came).wait_recv()
                    if step < 4 - way:
                        self.near(half, way, step + 1, came).start()
                    self.first_hop(half, came)

    def arrive_and_forward(self, hop, part):
        for half in range(2):
            for way in range(2):
                row = wrap(self.big[half] - hop * (1 - 2 * way))
                self.far(half, way, hop, part, row, part * 4, 4).wait_recv()

                @pl.when((hop < 3) | (part == way))
                def _():
                    self.far(half, way, hop + 1, part, row, part * 4, 4).start()

    def arrive_last(self):
        for half in range(2):
            for way in range(2):
                row = wrap(self.big[half] + 4)
                self.far(half, way, 4, way, row, way * 4, 4).wait_recv()

    def finish(self):
        for half in range(2):
            for way in range(2):
                for step in range(1, 5 - way):
                    self.near(half, way, step, self.small[half]).wait_send()
                for hop in range(1, 4):
                    for part in range(2):
                        self.far(half, way, hop, part, self.big[half], part * 4, 4).wait_send()
                self.far(half, way, 4, way, self.big[half], way * 4, 4).wait_send()


def kernel(tok_hbm, gain_ref, wq_hbm, wk_hbm, wv_hbm, order_ref, doc_ref, table_ref, out_ref,
           tok, normed, other, wq, wk, wv, w0, w1, part, kv_out, q_out, kv_in, q_in,
           kv0, kv1, meta_out, meta_in, meta_s, q_ref, qpos, qlo, run_max, acc, bias,
           load_sem, meta_sem, seed_send, seed_recv, tok_send, tok_recv, part_send, part_recv,
           w_ns, w_nr, w_fs, w_fr, kv_ns, kv_nr, kv_fs, kv_fr):
    ctx, y, section = lax.axis_index("ctx"), lax.axis_index("dp"), lax.axis_index("section")
    x, z = lax.rem(ctx, RING), ctx // RING
    mate = y + 1 - 2 * lax.rem(y, 2)
    twin = lax.rem(y + 2, 4)
    after, before = lax.rem(section + 1, 4), lax.rem(section + 3, 4)

    loads = [
        pltpu.make_async_copy(tok_hbm.at[0, 0], tok, load_sem.at[0]),
        pltpu.make_async_copy(wq_hbm.at[0], wq, load_sem.at[1]),
        pltpu.make_async_copy(wk_hbm.at[0], wk, load_sem.at[2]),
        pltpu.make_async_copy(wv_hbm.at[0], wv, load_sem.at[3]),
    ]
    for load in loads:
        load.start()

    weights = Gather((w0, w1), 16, x, z, w_ns, w_nr, w_fs, w_fr)
    kvs = Gather((kv0, kv1), BLOCK, x, z, kv_ns, kv_nr, kv_fs, kv_fr)

    barrier = pltpu.get_barrier_semaphore()
    greeted = [weights.small_device(half, by) for half in range(2) for by in (1, -1)]
    greeted += [{"dp": mate}, {"dp": twin}]
    greeted += [{"section": before}, {"section": before, "dp": mate}]
    for device in greeted:
        pl.semaphore_signal(barrier, inc=1, device_id=device, device_id_type=MESH)
    pl.semaphore_wait(barrier, len(greeted))

    rows0 = pl.ds(pl.multiple_of((z * RING + x) * 16, 16), 16)
    rows1 = pl.ds(pl.multiple_of((x * RING + z) * 16, 16), 16)

    def seed(number, src, dst):
        return pltpu.make_async_remote_copy(
            src_ref=src, dst_ref=dst, send_sem=seed_send.at[number],
            recv_sem=seed_recv.at[number], device_id={"dp": twin}, device_id_type=MESH)

    seeds = [
        seed(0, wq_hbm.at[0, rows0, pl.ds(0, 384)], w0.at[rows0, :]),
        seed(1, wq_hbm.at[0, rows1, pl.ds(384, 128)], w1.at[rows1, pl.ds(0, 128)]),
        seed(2, wk_hbm.at[0, rows1, :], w1.at[rows1, pl.ds(128, 128)]),
        seed(3, wv_hbm.at[0, rows1, :], w1.at[rows1, pl.ds(256, 128)]),
    ]
    for copy in seeds:
        copy.start()

    meta_out[...] = jnp.zeros_like(meta_out)
    meta_out[0:1, :] = order_ref[...]
    documents = doc_ref[...]
    for number in range(1, 4):
        count = jnp.sum(jnp.where(documents < number, 1.0, 0.0), axis=1, keepdims=True)
        meta_out[number:number + 1, :] = jnp.broadcast_to(count, (1, 128)).astype(jnp.int32)
    meta_copy = pltpu.make_async_remote_copy(
        src_ref=meta_out, dst_ref=meta_in, send_sem=meta_sem.at[0], recv_sem=meta_sem.at[1],
        device_id={"section": after}, device_id_type=MESH)
    meta_copy.start()

    loads[0].wait()
    wide = tok.shape[1] // 4
    square = jnp.zeros((128, 128), F32)
    for column in range(0, tok.shape[1], 128):
        piece = tok[:, column:column + 128].astype(F32)
        square = square + piece * piece
    mean = jnp.sum(square, axis=1, keepdims=True) * (1.0 / tok.shape[1])
    scale = lax.rsqrt(mean + EPSILON)

    def quarter(number):
        columns = pl.ds(pl.multiple_of(number * wide, wide), wide)
        value = tok[:, columns].astype(F32) * scale * gain_ref[:, columns]
        normed[number] = value.astype(BF16)

    def token_copy(slot, number):
        return pltpu.make_async_remote_copy(
            src_ref=normed.at[number], dst_ref=other.at[slot], send_sem=tok_send.at[slot],
            recv_sem=tok_recv.at[slot], device_id={"dp": mate}, device_id_type=MESH)

    token_copies = [token_copy(0, mate), token_copy(1, 3 - y)]
    quarter(mate)
    token_copies[0].start()
    quarter(3 - y)
    token_copies[1].start()

    for copy in seeds:
        copy.wait_recv()
    weights.begin()
    quarter(y)
    quarter(twin)
    weights.near_steps()

    for load in loads[1:]:
        load.wait()

    def own_rows(who, value):
        part[who, :, 0:512] = jnp.dot(value, wq[...], preferred_element_type=F32)
        part[who, :, 512:640] = jnp.dot(value, wk[...], preferred_element_type=F32)
        part[who, :, 640:768] = jnp.dot(value, wv[...], preferred_element_type=F32)

    def forward_step(t, carry):
        weights.arrive_and_forward(t // 2 + 1, lax.rem(t, 2))
        return carry

    own_rows(0, normed[y])
    lax.fori_loop(0, 3, forward_step, 0)
    token_copies[0].wait_recv()
    own_rows(1, other[0])
    lax.fori_loop(3, 6, forward_step, 0)
    token_copies[1].wait_recv()
    weights.arrive_last()

    def part_copy(number, who, src, dst):
        device = {"section": after} if who == 0 else {"section": after, "dp": mate}
        return pltpu.make_async_remote_copy(
            src_ref=src.at[who], dst_ref=dst.at[who], send_sem=part_send.at[number],
            recv_sem=part_recv.at[number], device_id=device, device_id_type=MESH)

    part_copies = [part_copy(who, who, kv_out, kv_in) for who in range(2)]
    part_copies += [part_copy(2 + who, who, q_out, q_in) for who in range(2)]
    for who in (1, 0):
        value = normed[twin] if who == 0 else other[1]
        rest = jnp.dot(value, w1[...], preferred_element_type=F32)
        kv_out[who] = (part[who, :, 512:768] + rest[:, 128:384]).astype(BF16)
        part_copies[who].start()
        q_out[who, :, 384:512] = (part[who, :, 384:512] + rest[:, 0:128]).astype(BF16)
    for who in (1, 0):
        value = normed[twin] if who == 0 else other[1]
        rest = jnp.dot(value, w0[...], preferred_element_type=F32)
        q_out[who, :, 0:384] = (part[who, :, 0:384] + rest).astype(BF16)
        part_copies[2 + who].start()

    meta_copy.wait_recv()
    to_scalars = pltpu.make_async_copy(meta_in, meta_s, load_sem.at[4])
    to_scalars.start()
    to_scalars.wait()

    def block_of(slot_z, slot_x, half):
        return meta_s[0, (slot_z * RING + slot_x) * 2 + half]

    lane = lax.broadcasted_iota(jnp.int32, (BLOCK, HEAD), 1)
    sign = jnp.where(lane < HEAD // 2, -1.0, 1.0)
    fine_cos = table_ref[256:320, :]
    fine_sin = table_ref[320:384, :]
    turns = []
    for half in range(2):
        block = block_of(z, x, half)
        coarse_cos = table_ref[pl.ds(block, 1), :]
        coarse_sin = table_ref[pl.ds(block + 128, 1), :]
        cosine = coarse_cos * fine_cos - coarse_sin * fine_sin
        sine = (coarse_sin * fine_cos + coarse_cos * fine_sin) * sign
        turns.append((cosine, sine))
        position = block * BLOCK + lax.broadcasted_iota(jnp.int32, (BLOCK, 128), 0)
        low = jnp.zeros((BLOCK, 128), jnp.int32)
        for number in range(1, 4):
            start = meta_in[number:number + 1, :]
            low = jnp.maximum(low, jnp.where(start <= position, start, 0))
        qpos[half * BLOCK:(half + 1) * BLOCK, :] = position
        qlo[half * BLOCK:(half + 1) * BLOCK, :] = low

    def turned(value, half):
        cosine, sine = turns[half]
        return value * cosine + pltpu.roll(value, HEAD // 2, 1) * sine

    for copy in part_copies[:2]:
        copy.wait_recv()
    for half in range(2):
        rows = slice(half * BLOCK, (half + 1) * BLOCK)
        both = kv_in[0, rows, :].astype(F32) + kv_in[1, rows, :].astype(F32)
        big, small = (z, x) if half == 0 else (x, z)
        slot = pl.ds(pl.multiple_of((big * RING + small) * BLOCK, BLOCK), BLOCK)
        buffer = kv0 if half == 0 else kv1
        buffer[slot, 0:128] = turned(both[:, 0:128], half).astype(BF16)
        buffer[slot, 128:256] = both[:, 128:256].astype(BF16)
    kvs.begin()

    run_max[...] = jnp.full(run_max.shape, FLOOR, F32)
    acc[...] = jnp.zeros_like(acc)
    kvs.near_steps()
    for copy in part_copies[2:]:
        copy.wait_recv()
    for half in range(2):
        rows = slice(half * BLOCK, (half + 1) * BLOCK)
        for head in range(4):
            columns = slice(head * HEAD, (head + 1) * HEAD)
            both = q_in[0, rows, columns].astype(F32) + q_in[1, rows, columns].astype(F32)
            q_ref[head, rows, :] = turned(both, half).astype(BF16)

    scaling = math.log2(math.e) * HEAD ** -0.5
    lanes = lax.broadcasted_iota(jnp.int32, (1, 128), 1)
    inner = lax.rem(lanes, BLOCK)
    first = lanes < BLOCK

    def tile(t, carry):
        hop = (t + 1) // 2
        one_row = (t == 0) | (t == 7)
        half_row = lax.rem(t + 1, 2)

        @pl.when((t > 0) & (t < 7))
        def _():
            kvs.arrive_and_forward(hop, half_row)

        @pl.when(t == 7)
        def _():
            kvs.arrive_last()

        keys, values = [], []
        for half in range(2):
            for way in range(2):
                big = wrap(kvs.big[half] - hop * (1 - 2 * way))
                small = 4 * jnp.where(one_row, way, half_row)
                begin = pl.multiple_of((big * RING + small) * BLOCK, 4 * BLOCK)
                buffer = kv0 if half == 0 else kv1
                both = buffer[pl.ds(begin, 4 * BLOCK), :]
                keys.append(both[:, 0:128])
                values.append(both[:, 128:256])
                for pair in range(2):
                    numbers = []
                    for k in range(2):
                        inside = small + 2 * pair + k
                        if half == 0:
                            numbers.append(block_of(big, inside, 0))
                        else:
                            numbers.append(block_of(inside, big, 1))
                    position = jnp.where(first, numbers[0], numbers[1]) * BLOCK + inner
                    column = (half * 2 + way) * 256 + pair * 128
                    allowed = (position <= qpos[...]) & (position >= qlo[...])
                    bias[:, column:column + 128] = jnp.where(allowed, 0.0, MASKED)
        key = jnp.concatenate(keys, axis=0)
        value = jnp.concatenate(values, axis=0)
        value = jnp.concatenate([value, jnp.ones_like(value)], axis=1)
        for head in range(4):
            scores = lax.dot_general(q_ref[head], key, (((1,), (1,)), ((), ())),
                                     preferred_element_type=F32)
            scores = scores * scaling + bias[...]
            old = run_max[head]
            new = jnp.maximum(old, jnp.max(scores, axis=1, keepdims=True))
            run_max[head] = new
            probs = jnp.exp2(scores - new[:, 0:1]).astype(BF16)
            factor = jnp.exp2(old - new)
            got = jnp.dot(probs, value, preferred_element_type=F32)
            acc[head, :, 0:128] = acc[head, :, 0:128] * factor + got[:, 0:128]
            acc[head, :, 128:256] = acc[head, :, 128:256] * factor + got[:, 128:256]
        return carry

    lax.fori_loop(0, 8, tile, 0)

    for head in range(4):
        result = acc[head, :, 0:128] / acc[head, :, 128:256]
        out_ref[:, head * HEAD:(head + 1) * HEAD] = result.astype(BF16)

    for copy in seeds:
        copy.wait_send()
    meta_copy.wait_send()
    for copy in token_copies + part_copies:
        copy.wait_send()
    weights.finish()
    kvs.finish()


def local(tokens, norm_gain, query_weight, key_weight, value_weight, block_order, doc_ids):
    width = tokens.shape[3]
    deep = width // 4
    table = jnp.asarray(rope_tables())
    anywhere = pl.BlockSpec(memory_space=pl.ANY)
    vmem = pl.BlockSpec(memory_space=pltpu.VMEM)
    dma = pltpu.SemaphoreType.DMA
    out = pl.pallas_call(
        kernel,
        out_shape=jax.ShapeDtypeStruct((128, 512), BF16),
        in_specs=[anywhere, vmem, anywhere, anywhere, anywhere, vmem, vmem, vmem],
        out_specs=vmem,
        scratch_shapes=[
            pltpu.VMEM((128, width), BF16),
            pltpu.VMEM((4, 128, deep), BF16),
            pltpu.VMEM((2, 128, deep), BF16),
            pltpu.VMEM((deep, 512), BF16),
            pltpu.VMEM((deep, 128), BF16),
            pltpu.VMEM((deep, 128), BF16),
            pltpu.VMEM((deep, 384), BF16),
            pltpu.VMEM((deep, 384), BF16),
            pltpu.VMEM((2, 128, 768), F32),
            pltpu.VMEM((2, 128, 256), BF16),
            pltpu.VMEM((2, 128, 512), BF16),
            pltpu.VMEM((2, 128, 256), BF16),
            pltpu.VMEM((2, 128, 512), BF16),
            pltpu.VMEM((64 * BLOCK, 256), BF16),
            pltpu.VMEM((64 * BLOCK, 256), BF16),
            pltpu.VMEM((8, 128), jnp.int32),
            pltpu.VMEM((8, 128), jnp.int32),
            pltpu.SMEM((8, 128), jnp.int32),
            pltpu.VMEM((4, 128, 128), BF16),
            pltpu.VMEM((128, 128), jnp.int32),
            pltpu.VMEM((128, 128), jnp.int32),
            pltpu.VMEM((4, 128, 128), F32),
            pltpu.VMEM((4, 128, 256), F32),
            pltpu.VMEM((128, 1024), F32),
            dma((5,)), dma((2,)), dma((4,)), dma((4,)), dma((2,)), dma((2,)), dma((4,)), dma((4,)),
            dma((2, 2, 4)), dma((2, 2, 4)), dma((2, 2, 4, 2)), dma((2, 2, 4, 2)),
            dma((2, 2, 4)), dma((2, 2, 4)), dma((2, 2, 4, 2)), dma((2, 2, 4, 2)),
        ],
        compiler_params=pltpu.CompilerParams(
            collective_id=0, has_side_effects=True, vmem_limit_bytes=40 * 1024 * 1024),
        name="relay_attention",
    )(tokens, norm_gain, query_weight, key_weight, value_weight, block_order[0], doc_ids[0], table)
    return out[None, None]


def solution(mesh):
    in_specs = (
        P("section", "dp", "ctx", None),
        P("section", None),
        P("section", "dp", None),
        P("section", "dp", None),
        P("section", "dp", None),
        P("section", "dp", None),
        P("section", "dp", None),
    )
    out_specs = P("section", "dp", "ctx", None)
    return jax.shard_map(local, mesh=mesh, in_specs=in_specs, out_specs=out_specs, check_vma=False)
```

time: 430 us -> 100 us (0.23)
  the two profiles are of different devices: /device:TPU:32 before, /device:TPU:2 now
where the time goes in v1:
time: 100 us; the launch traced here: 99.9 us
  Pallas kernels  91.8 us (92%)
  local copies, waits for them, and re-layouts  8.06 us (8%)
    pallas_call x1, Pallas kernels, local(): pl.pallas_call(kernel, out_shape=jax.ShapeDtypeStruct((128, 512), BF16),...  91.8 us
    unnamed x17, local copies, waits for them, and re-layouts  8.06 us

profile of v1, /device:TPU:2, one launch (start us, length us, event | category | flops | bytes accessed | tf_op | source)
XLA Modules:
  0.0 99.9 jit_solution(11990093246422424894)
XLA Ops:
  0.0 0.0 copy-start.7
  0.0 0.7 copy-done.7
  0.7 0.0 copy-start
  0.7 1.2 %copy-done = bf16[1,1,128,4096]{3,2,1,0:T(8,128)(2,1)S(1)} copy-done((bf16[1,1,128,4096]{3,2,1,0:T(8,128)(2,1)S(1)}, bf16[1,1,128,4096]{3,2,1,0:T(8,128)(2,1)}, u32[]{:S(2)}) %copy-start) | copy-done | bytes 1048600
  1.9 0.0 copy-start.1
  1.9 1.2 %copy-done.1 = bf16[1,1024,512]{2,1,0:T(8,128)(2,1)S(1)} copy-done((bf16[1,1024,512]{2,1,0:T(8,128)(2,1)S(1)}, bf16[1,1024,512]{2,1,0:T(8,128)(2,1)}, u32[]{:S(2)}) %copy-start.1) | copy-done | bytes 1048600
  3.1 0.0 copy-start.2
  3.1 0.9 copy-done.2
  4.1 0.0 copy-start.3
  4.1 0.9 copy-done.3
  5.0 0.0 copy-start.4
  5.0 0.9 copy-done.4
  5.9 0.0 copy-start.5
  5.9 0.8 copy-done.5
  6.7 0.0 copy-start.6
  6.7 0.7 copy-done.6
  7.4 91.8 %relay_attention.1 = bf16[128,512]{1,0:T(8,128)(2,1)S(1)} custom-call(bf16[1,1,128,4096]{3,2,1,0:T(8,128)(2,1)S(1)} %copy-done, f32[1,4096]{1,0:T(1,128)S(1)} %copy-done.6, bf16[1,1024,512]{2,1,0:T(8,128)(2,1)S(1)} %copy-done.1, bf16[1,1024,128]{2,1,0:T(8,128)(2,1)S(1)} %copy-done.2, bf16[1,1024,128]{2,1,0:T(8,128)(2,1)S(1)} %copy-done.3, ...), custom_call_target="tpu_custom_call" | custom-call | tf_op jit(solution)/shard_map/relay_attention/pallas_call | solution.py:388
  99.2 0.7 copy.10
Async XLA Ops:
  0.0 0.7 copy-start.7
  0.7 1.2 %copy-start = (bf16[1,1,128,4096]{3,2,1,0:T(8,128)(2,1)S(1)}, bf16[1,1,128,4096]{3,2,1,0:T(8,128)(2,1)}, u32[]{:S(2)}) copy-start(bf16[1,1,128,4096]{3,2,1,0:T(8,128)(2,1)} %tok_hbm.1) | copy-start | bytes 3145732
  1.9 1.2 %copy-start.1 = (bf16[1,1024,512]{2,1,0:T(8,128)(2,1)S(1)}, bf16[1,1024,512]{2,1,0:T(8,128)(2,1)}, u32[]{:S(2)}) copy-start(bf16[1,1024,512]{2,1,0:T(8,128)(2,1)} %wq_hbm.1) | copy-start | bytes 3145732
  3.1 0.9 copy-start.2
  4.1 0.9 copy-start.3
  5.0 0.9 copy-start.4
  5.9 0.8 copy-start.5
  6.7 0.7 copy-start.6

commit v2 on v1

--- a/solution.py
+++ b/solution.py
@@ -33,9 +33,9 @@
     return lax.rem(i + 2 * RING, RING)
 
 
-class Gather:
-    def __init__(self, bufs, rows, x, z, near_send, near_recv, far_send, far_recv):
-        self.bufs, self.rows = bufs, rows
+class Plane:
+    def __init__(self, bufs, x, z, near_send, near_recv, far_send, far_recv):
+        self.bufs = bufs
         self.small = (x, z)
         self.big = (z, x)
         self.near_send, self.near_recv = near_send, near_recv
@@ -50,77 +50,133 @@
     def big_device(self, half, by):
         return self.small_device(1 - half, by)
 
-    def slots(self, half, big, small, count):
-        start = pl.multiple_of((big * RING + small) * self.rows, self.rows)
-        return self.bufs[half].at[pl.ds(start, count * self.rows), :]
-
-    def near(self, half, way, step, small):
-        ref = self.slots(half, self.big[half], small, 1)
-        return pltpu.make_async_remote_copy(
-            src_ref=ref, dst_ref=ref,
+
+class Spread(Plane):
+    def rows(self, half, big, small, begin=0, count=64):
+        start = (lax.rem(big, 4) * 4 + lax.rem(small, 4)) * 64 + begin
+        return self.bufs[half].at[pl.ds(pl.multiple_of(start, 32), count), :]
+
+    def near(self, half, number, small):
+        big = self.big[half]
+        if number < 2:
+            ref = self.rows(half, big, small)
+        else:
+            ref = self.rows(half, big, small, 32 * (number - 2), 32)
+        return pltpu.make_async_remote_copy(
+            src_ref=ref, dst_ref=ref, send_sem=self.near_send.at[half, number],
+            recv_sem=self.near_recv.at[half, number],
+            device_id=self.small_device(half, (1, -1, 2, -2)[number]), device_id_type=MESH)
+
+    def far(self, half, number, kind, big):
+        small = wrap(self.small[half] + (0, -1, 1, 2)[kind])
+        ref = self.rows(half, big, small)
+        by = (1, -1, 2 if kind < 2 else -2)[number]
+        return pltpu.make_async_remote_copy(
+            src_ref=ref, dst_ref=ref, send_sem=self.far_send.at[half, number, kind],
+            recv_sem=self.far_recv.at[half, number, kind],
+            device_id=self.big_device(half, by), device_id_type=MESH)
+
+    def far_sends(self, half, kind):
+        for number in (2, 0, 1):
+            self.far(half, number, kind, self.big[half]).start()
+
+    def begin(self, half):
+        for number in (2, 3, 0, 1):
+            self.near(half, number, self.small[half]).start()
+        self.far_sends(half, 0)
+
+    def near_steps(self):
+        for numbers, kind in (((0,), 1), ((1,), 2), ((2, 3), 3)):
+            for half in (1, 0):
+                for number in numbers:
+                    came = wrap(self.small[half] + (-1, 1, 2, 2)[number])
+                    self.near(half, number, came).wait_recv()
+                self.far_sends(half, kind)
+
+    def arrive(self, half):
+        for kind in range(4):
+            for number in range(3):
+                row = wrap(self.big[half] + (-1, 1, 2)[number])
+                self.far(half, number, kind, row).wait_recv()
+
+    def finish(self):
+        for half in range(2):
+            for number in range(4):
+                self.near(half, number, self.small[half]).wait_send()
+            for kind in range(4):
+                for number in range(3):
+                    self.far(half, number, kind, self.big[half]).wait_send()
+
+
+class Gather(Plane):
+    def slots(self, half, big, index, count):
+        start = pl.multiple_of((big * RING + index) * BLOCK, BLOCK)
+        return self.bufs[half].at[pl.ds(start, count * BLOCK), :]
+
+    def came(self, way, step):
+        return 2 * step - 1 + way if step else 0
+
+    def near(self, half, way, step):
+        jump = step if step < 3 else 1
+        held = self.came(way, step - 1) if step > 2 else 0
+        return pltpu.make_async_remote_copy(
+            src_ref=self.slots(half, self.big[half], held, 1),
+            dst_ref=self.slots(half, self.big[half], self.came(way, step), 1),
             send_sem=self.near_send.at[half, way, step - 1],
             recv_sem=self.near_recv.at[half, way, step - 1],
-            device_id=self.small_device(half, 1 - 2 * way), device_id_type=MESH)
-
-    def far(self, half, way, hop, part, big, small, count):
-        ref = self.slots(half, big, small, count)
+            device_id=self.small_device(half, jump * (1 - 2 * way)), device_id_type=MESH)
+
+    def far(self, half, way, hop, part, big, index, count):
+        ref = self.slots(half, big, index, count)
         return pltpu.make_async_remote_copy(
             src_ref=ref, dst_ref=ref,
             send_sem=self.far_send.at[half, way, hop - 1, part],
             recv_sem=self.far_recv.at[half, way, hop - 1, part],
             device_id=self.big_device(half, 1 - 2 * way), device_id_type=MESH)
 
-    def first_hop(self, half, small):
+    def first_hop(self, half, index):
         for way in range(2):
-            self.far(half, way, 1, small // 4, self.big[half], small, 1).start()
-
-    def begin(self):
+            self.far(half, way, 1, index // 2, self.big[half], index, 1).start()
+
+    def begin(self, half):
+        for step in range(1, 3):
+            for way in range(2):
+                self.near(half, way, step).start()
+            if step == 1:
+                self.first_hop(half, 0)
+
+    def near_step(self, step):
         for half in range(2):
             for way in range(2):
-                self.near(half, way, 1, self.small[half]).start()
-            self.first_hop(half, self.small[half])
-
-    def near_steps(self):
-        for step in range(1, 5):
-            for half in range(2):
-                for way in range(2):
-                    if step == 4 and way == 1:
-                        continue
-                    came = wrap(self.small[half] - step * (1 - 2 * way))
-                    self.near(half, way, step, came).wait_recv()
-                    if step < 4 - way:
-                        self.near(half, way, step + 1, came).start()
-                    self.first_hop(half, came)
-
-    def arrive_and_forward(self, hop, part):
+                if step + way < 5:
+                    self.near(half, way, step).wait_recv()
+                    if step in (2, 3) and step + 1 + way < 5:
+                        self.near(half, way, step + 1).start()
+                    self.first_hop(half, self.came(way, step))
+
+    def arrive(self, hop, part):
         for half in range(2):
             for way in range(2):
+                if hop == 4 and part // 2 != way:
+                    continue
                 row = wrap(self.big[half] - hop * (1 - 2 * way))
-                self.far(half, way, hop, part, row, part * 4, 4).wait_recv()
-
-                @pl.when((hop < 3) | (part == way))
-                def _():
-                    self.far(half, way, hop + 1, part, row, part * 4, 4).start()
-
-    def arrive_last(self):
-        for half in range(2):
-            for way in range(2):
-                row = wrap(self.big[half] + 4)
-                self.far(half, way, 4, way, row, way * 4, 4).wait_recv()
+                self.far(half, way, hop, part, row, part * 2, 2).wait_recv()
+                if hop < 3 or (hop == 3 and part // 2 == way):
+                    self.far(half, way, hop + 1, part, row, part * 2, 2).start()
 
     def finish(self):
         for half in range(2):
             for way in range(2):
                 for step in range(1, 5 - way):
-                    self.near(half, way, step, self.small[half]).wait_send()
-                for hop in range(1, 4):
-                    for part in range(2):
-                        self.far(half, way, hop, part, self.big[half], part * 4, 4).wait_send()
-                self.far(half, way, 4, way, self.big[half], way * 4, 4).wait_send()
-
-
-def kernel(tok_hbm, gain_ref, wq_hbm, wk_hbm, wv_hbm, order_ref, doc_ref, table_ref, out_ref,
-           tok, normed, other, wq, wk, wv, w0, w1, part, kv_out, q_out, kv_in, q_in,
+                    self.near(half, way, step).wait_send()
+                for hop in range(1, 5):
+                    for part in range(4):
+                        if hop < 4 or part // 2 == way:
+                            self.far(half, way, hop, part, self.big[half], part * 2, 2).wait_send()
+
+
+def kernel(tok_hbm, gain_hbm, wq_hbm, wk_hbm, wv_hbm, order_hbm, doc_hbm, table_hbm, out_ref,
+           gain_ref, order_ref, doc_ref, table_ref, tok, normed, other, wq, wk, wv, w0, w1, part, kv_out, q_out, kv_in, q_in,
            kv0, kv1, meta_out, meta_in, meta_s, q_ref, qpos, qlo, run_max, acc, bias,
            load_sem, meta_sem, seed_send, seed_recv, tok_send, tok_recv, part_send, part_recv,
            w_ns, w_nr, w_fs, w_fr, kv_ns, kv_nr, kv_fs, kv_fr):
@@ -130,28 +186,34 @@
     twin = lax.rem(y + 2, 4)
     after, before = lax.rem(section + 1, 4), lax.rem(section + 3, 4)
 
+    small_loads = [
+        pltpu.make_async_copy(order_hbm.at[0], order_ref, load_sem.at[5]),
+        pltpu.make_async_copy(doc_hbm.at[0], doc_ref, load_sem.at[6]),
+        pltpu.make_async_copy(gain_hbm, gain_ref, load_sem.at[7]),
+        pltpu.make_async_copy(table_hbm, table_ref, load_sem.at[8]),
+    ]
     loads = [
         pltpu.make_async_copy(tok_hbm.at[0, 0], tok, load_sem.at[0]),
         pltpu.make_async_copy(wq_hbm.at[0], wq, load_sem.at[1]),
         pltpu.make_async_copy(wk_hbm.at[0], wk, load_sem.at[2]),
         pltpu.make_async_copy(wv_hbm.at[0], wv, load_sem.at[3]),
     ]
-    for load in loads:
+    for load in loads[:1] + small_loads + loads[1:]:
         load.start()
 
-    weights = Gather((w0, w1), 16, x, z, w_ns, w_nr, w_fs, w_fr)
-    kvs = Gather((kv0, kv1), BLOCK, x, z, kv_ns, kv_nr, kv_fs, kv_fr)
+    weights = Spread((w0, w1), x, z, w_ns, w_nr, w_fs, w_fr)
+    kvs = Gather((kv0, kv1), x, z, kv_ns, kv_nr, kv_fs, kv_fr)
 
     barrier = pltpu.get_barrier_semaphore()
-    greeted = [weights.small_device(half, by) for half in range(2) for by in (1, -1)]
+    greeted = [weights.small_device(half, by) for half in range(2)
+               for by in (1, -1, 2, -2)]
     greeted += [{"dp": mate}, {"dp": twin}]
     greeted += [{"section": before}, {"section": before, "dp": mate}]
     for device in greeted:
         pl.semaphore_signal(barrier, inc=1, device_id=device, device_id_type=MESH)
-    pl.semaphore_wait(barrier, len(greeted))
-
-    rows0 = pl.ds(pl.multiple_of((z * RING + x) * 16, 16), 16)
-    rows1 = pl.ds(pl.multiple_of((x * RING + z) * 16, 16), 16)
+
+    rows0 = pl.ds(pl.multiple_of((lax.rem(z, 4) * 4 + lax.rem(x, 4)) * 64, 64), 64)
+    rows1 = pl.ds(pl.multiple_of((lax.rem(x, 4) * 4 + lax.rem(z, 4)) * 64, 64), 64)
 
     def seed(number, src, dst):
         return pltpu.make_async_remote_copy(
@@ -164,10 +226,10 @@
         seed(2, wk_hbm.at[0, rows1, :], w1.at[rows1, pl.ds(128, 128)]),
         seed(3, wv_hbm.at[0, rows1, :], w1.at[rows1, pl.ds(256, 128)]),
     ]
-    for copy in seeds:
-        copy.start()
 
     meta_out[...] = jnp.zeros_like(meta_out)
+    small_loads[0].wait()
+    small_loads[1].wait()
     meta_out[0:1, :] = order_ref[...]
     documents = doc_ref[...]
     for number in range(1, 4):
@@ -176,9 +238,9 @@
     meta_copy = pltpu.make_async_remote_copy(
         src_ref=meta_out, dst_ref=meta_in, send_sem=meta_sem.at[0], recv_sem=meta_sem.at[1],
         device_id={"section": after}, device_id_type=MESH)
-    meta_copy.start()
 
     loads[0].wait()
+    small_loads[2].wait()
     wide = tok.shape[1] // 4
     square = jnp.zeros((128, 128), F32)
     for column in range(0, tok.shape[1], 128):
@@ -199,17 +261,13 @@
 
     token_copies = [token_copy(0, mate), token_copy(1, 3 - y)]
     quarter(mate)
-    token_copies[0].start()
     quarter(3 - y)
-    token_copies[1].start()
-
-    for copy in seeds:
-        copy.wait_recv()
-    weights.begin()
+
+    pl.semaphore_wait(barrier, len(greeted))
+    for copy in seeds[1:] + seeds[:1] + token_copies + [meta_copy]:
+        copy.start()
     quarter(y)
     quarter(twin)
-    weights.near_steps()
-
     for load in loads[1:]:
         load.wait()
 
@@ -218,17 +276,17 @@
         part[who, :, 512:640] = jnp.dot(value, wk[...], preferred_element_type=F32)
         part[who, :, 640:768] = jnp.dot(value, wv[...], preferred_element_type=F32)
 
-    def forward_step(t, carry):
-        weights.arrive_and_forward(t // 2 + 1, lax.rem(t, 2))
-        return carry
-
     own_rows(0, normed[y])
-    lax.fori_loop(0, 3, forward_step, 0)
+    for copy in seeds[1:]:
+        copy.wait_recv()
+    weights.begin(1)
+    seeds[0].wait_recv()
+    weights.begin(0)
+    weights.near_steps()
     token_copies[0].wait_recv()
     own_rows(1, other[0])
-    lax.fori_loop(3, 6, forward_step, 0)
     token_copies[1].wait_recv()
-    weights.arrive_last()
+    weights.arrive(1)
 
     def part_copy(number, who, src, dst):
         device = {"section": after} if who == 0 else {"section": after, "dp": mate}
@@ -244,6 +302,7 @@
         kv_out[who] = (part[who, :, 512:768] + rest[:, 128:384]).astype(BF16)
         part_copies[who].start()
         q_out[who, :, 384:512] = (part[who, :, 384:512] + rest[:, 0:128]).astype(BF16)
+    weights.arrive(0)
     for who in (1, 0):
         value = normed[twin] if who == 0 else other[1]
         rest = jnp.dot(value, w0[...], preferred_element_type=F32)
@@ -251,6 +310,7 @@
         part_copies[2 + who].start()
 
     meta_copy.wait_recv()
+    small_loads[3].wait()
     to_scalars = pltpu.make_async_copy(meta_in, meta_s, load_sem.at[4])
     to_scalars.start()
     to_scalars.wait()
@@ -287,16 +347,23 @@
     for half in range(2):
         rows = slice(half * BLOCK, (half + 1) * BLOCK)
         both = kv_in[0, rows, :].astype(F32) + kv_in[1, rows, :].astype(F32)
-        big, small = (z, x) if half == 0 else (x, z)
-        slot = pl.ds(pl.multiple_of((big * RING + small) * BLOCK, BLOCK), BLOCK)
+        big = z if half == 0 else x
+        slot = pl.ds(pl.multiple_of(big * RING * BLOCK, BLOCK), BLOCK)
         buffer = kv0 if half == 0 else kv1
         buffer[slot, 0:128] = turned(both[:, 0:128], half).astype(BF16)
         buffer[slot, 128:256] = both[:, 128:256].astype(BF16)
-    kvs.begin()
+    kvs.begin(0)
+    kvs.begin(1)
 
     run_max[...] = jnp.full(run_max.shape, FLOOR, F32)
     acc[...] = jnp.zeros_like(acc)
-    kvs.near_steps()
+    kvs.near_step(1)
+    kvs.near_step(2)
+    kvs.arrive(1, 0)
+    kvs.near_step(3)
+    kvs.arrive(1, 1)
+    kvs.arrive(2, 0)
+    kvs.near_step(4)
     for copy in part_copies[2:]:
         copy.wait_recv()
     for half in range(2):
@@ -312,17 +379,17 @@
     first = lanes < BLOCK
 
     def tile(t, carry):
-        hop = (t + 1) // 2
         one_row = (t == 0) | (t == 7)
-        half_row = lax.rem(t + 1, 2)
-
-        @pl.when((t > 0) & (t < 7))
-        def _():
-            kvs.arrive_and_forward(hop, half_row)
-
-        @pl.when(t == 7)
-        def _():
-            kvs.arrive_last()
+        hop = jnp.where(t == 0, 0, jnp.where((t == 1) | (t == 3), 1, jnp.where(
+            (t == 2) | (t == 5), 2, jnp.where(t == 7, 4, 3))))
+        half_row = jnp.where((t == 3) | (t == 5) | (t == 6), 1, 0)
+        due = {1: [(1, 2)], 2: [(2, 1), (3, 0), (1, 3)], 3: [(2, 2)], 4: [(3, 1), (2, 3)],
+               5: [(3, 2)], 6: [(3, 3)], 7: [(4, 0), (4, 1), (4, 2), (4, 3)]}
+        for number, pieces in due.items():
+            @pl.when(t == number)
+            def _(pieces=pieces):
+                for piece in pieces:
+                    kvs.arrive(*piece)
 
         keys, values = [], []
         for half in range(2):
@@ -337,7 +404,9 @@
                 for pair in range(2):
                     numbers = []
                     for k in range(2):
-                        inside = small + 2 * pair + k
+                        index = small + 2 * pair + k
+                        offset = (index + 1) // 2 * (1 - 2 * lax.rem(index, 2))
+                        inside = wrap(kvs.small[half] + offset)
                         if half == 0:
                             numbers.append(block_of(big, inside, 0))
                         else:
@@ -382,15 +451,19 @@
     width = tokens.shape[3]
     deep = width // 4
     table = jnp.asarray(rope_tables())
-    anywhere = pl.BlockSpec(memory_space=pl.ANY)
+    hbm = pl.BlockSpec(memory_space=pltpu.HBM)
     vmem = pl.BlockSpec(memory_space=pltpu.VMEM)
     dma = pltpu.SemaphoreType.DMA
     out = pl.pallas_call(
         kernel,
         out_shape=jax.ShapeDtypeStruct((128, 512), BF16),
-        in_specs=[anywhere, vmem, anywhere, anywhere, anywhere, vmem, vmem, vmem],
+        in_specs=[hbm] * 8,
         out_specs=vmem,
         scratch_shapes=[
+            pltpu.VMEM((1, width), F32),
+            pltpu.VMEM((1, 128), jnp.int32),
+            pltpu.VMEM((1, doc_ids.shape[2]), jnp.int32),
+            pltpu.VMEM(table.shape, F32),
             pltpu.VMEM((128, width), BF16),
             pltpu.VMEM((4, 128, deep), BF16),
             pltpu.VMEM((2, 128, deep), BF16),
@@ -415,14 +488,14 @@
             pltpu.VMEM((4, 128, 128), F32),
             pltpu.VMEM((4, 128, 256), F32),
             pltpu.VMEM((128, 1024), F32),
-            dma((5,)), dma((2,)), dma((4,)), dma((4,)), dma((2,)), dma((2,)), dma((4,)), dma((4,)),
-            dma((2, 2, 4)), dma((2, 2, 4)), dma((2, 2, 4, 2)), dma((2, 2, 4, 2)),
-            dma((2, 2, 4)), dma((2, 2, 4)), dma((2, 2, 4, 2)), dma((2, 2, 4, 2)),
+            dma((9,)), dma((2,)), dma((4,)), dma((4,)), dma((2,)), dma((2,)), dma((4,)), dma((4,)),
+            dma((2, 4)), dma((2, 4)), dma((2, 3, 4)), dma((2, 3, 4)),
+            dma((2, 2, 4)), dma((2, 2, 4)), dma((2, 2, 4, 4)), dma((2, 2, 4, 4)),
         ],
         compiler_params=pltpu.CompilerParams(
-            collective_id=0, has_side_effects=True, vmem_limit_bytes=40 * 1024 * 1024),
+            collective_id=0, has_side_effects=True, vmem_limit_bytes=63 * 1024 * 1024),
         name="relay_attention",
-    )(tokens, norm_gain, query_weight, key_weight, value_weight, block_order[0], doc_ids[0], table)
+    )(tokens, norm_gain, query_weight, key_weight, value_weight, block_order, doc_ids, table)
     return out[None, None]
 
 

time: 100 us -> 83 us (0.83)
  the two profiles are of different devices: /device:TPU:2 before, /device:TPU:114 now
where the time goes in v2:
time: 83 us; the launch traced here: 82.9 us
  Pallas kernels  81.3 us (98%)
  local copies, waits for them, and re-layouts  1.57 us (2%)
    pallas_call x1, Pallas kernels, local(): pl.pallas_call(kernel, out_shape=jax.ShapeDtypeStruct((128, 512), BF16),...  81.3 us

profile of v2, /device:TPU:114, one launch (start us, length us, event | category | flops | bytes accessed | tf_op | source)
XLA Modules:
  0.0 82.9 jit_solution(14204073655016367058)
XLA Ops:
  0.0 81.3 %relay_attention.1 = bf16[128,512]{1,0:T(8,128)(2,1)} custom-call(bf16[1,1,128,4096]{3,2,1,0:T(8,128)(2,1)} %tok_hbm.1, f32[1,4096]{1,0:T(1,128)} %gain_hbm.1, bf16[1,1024,512]{2,1,0:T(8,128)(2,1)} %wq_hbm.1, bf16[1,1024,128]{2,1,0:T(8,128)(2,1)} %wk_hbm.1, bf16[1,1024,128]{2,1,0:T(8,128)(2,1)} %wv_hbm.1, s32[1,1,128]{2,1,0:T(1,128)} %order_hbm.1, ...), custom_call_target="tpu_custom_call" | custom-call | tf_op jit(solution)/shard_map/relay_attention/pallas_call | solution.py:457
  81.3 1.6 %copy.10 = bf16[1,1,128,512]{3,2,1,0:T(8,128)(2,1)} copy(bf16[1,1,128,512]{3,2,1,0:T(8,128)(2,1)} %bitcast.1) | data formatting | bytes 262144

commit v3 on v2

--- a/solution.py
+++ b/solution.py
@@ -164,22 +164,22 @@
                 if hop < 3 or (hop == 3 and part // 2 == way):
                     self.far(half, way, hop + 1, part, row, part * 2, 2).start()
 
-    def finish(self):
+    def drain(self, hops, near=False):
         for half in range(2):
             for way in range(2):
-                for step in range(1, 5 - way):
+                for step in range(1, 5 - way if near else 1):
                     self.near(half, way, step).wait_send()
-                for hop in range(1, 5):
+                for hop in hops:
                     for part in range(4):
                         if hop < 4 or part // 2 == way:
                             self.far(half, way, hop, part, self.big[half], part * 2, 2).wait_send()
 
 
 def kernel(tok_hbm, gain_hbm, wq_hbm, wk_hbm, wv_hbm, order_hbm, doc_hbm, table_hbm, out_ref,
-           gain_ref, order_ref, doc_ref, table_ref, tok, normed, other, wq, wk, wv, w0, w1, part, kv_out, q_out, kv_in, q_in,
+           gain_ref, order_ref, doc_ref, table_ref, tok, normed, other, wq, wk, wv, wk_g, wv_g, wq0_g, wq1_g, part, kv_out, q_out, kv_in, q_in,
            kv0, kv1, meta_out, meta_in, meta_s, q_ref, qpos, qlo, run_max, acc, bias,
            load_sem, meta_sem, seed_send, seed_recv, tok_send, tok_recv, part_send, part_recv,
-           w_ns, w_nr, w_fs, w_fr, kv_ns, kv_nr, kv_fs, kv_fr):
+           w_ns, w_nr, w_fs, w_fr, wq_ns, wq_nr, wq_fs, wq_fr, kv_ns, kv_nr, kv_fs, kv_fr):
     ctx, y, section = lax.axis_index("ctx"), lax.axis_index("dp"), lax.axis_index("section")
     x, z = lax.rem(ctx, RING), ctx // RING
     mate = y + 1 - 2 * lax.rem(y, 2)
@@ -201,11 +201,12 @@
     for load in loads[:1] + small_loads + loads[1:]:
         load.start()
 
-    weights = Spread((w0, w1), x, z, w_ns, w_nr, w_fs, w_fr)
+    kv_weights = Spread((wk_g, wv_g), x, z, w_ns, w_nr, w_fs, w_fr)
+    q_weights = Spread((wq0_g, wq1_g), x, z, wq_ns, wq_nr, wq_fs, wq_fr)
     kvs = Gather((kv0, kv1), x, z, kv_ns, kv_nr, kv_fs, kv_fr)
 
     barrier = pltpu.get_barrier_semaphore()
-    greeted = [weights.small_device(half, by) for half in range(2)
+    greeted = [kvs.small_device(half, by) for half in range(2)
                for by in (1, -1, 2, -2)]
     greeted += [{"dp": mate}, {"dp": twin}]
     greeted += [{"section": before}, {"section": before, "dp": mate}]
@@ -221,10 +222,10 @@
             recv_sem=seed_recv.at[number], device_id={"dp": twin}, device_id_type=MESH)
 
     seeds = [
-        seed(0, wq_hbm.at[0, rows0, pl.ds(0, 384)], w0.at[rows0, :]),
-        seed(1, wq_hbm.at[0, rows1, pl.ds(384, 128)], w1.at[rows1, pl.ds(0, 128)]),
-        seed(2, wk_hbm.at[0, rows1, :], w1.at[rows1, pl.ds(128, 128)]),
-        seed(3, wv_hbm.at[0, rows1, :], w1.at[rows1, pl.ds(256, 128)]),
+        seed(0, wk_hbm.at[0, rows0, :], wk_g.at[rows0, :]),
+        seed(1, wv_hbm.at[0, rows1, :], wv_g.at[rows1, :]),
+        seed(2, wq_hbm.at[0, rows0, pl.ds(0, 256)], wq0_g.at[rows0, :]),
+        seed(3, wq_hbm.at[0, rows1, pl.ds(256, 256)], wq1_g.at[rows1, :]),
     ]
 
     meta_out[...] = jnp.zeros_like(meta_out)
@@ -264,7 +265,7 @@
     quarter(3 - y)
 
     pl.semaphore_wait(barrier, len(greeted))
-    for copy in seeds[1:] + seeds[:1] + token_copies + [meta_copy]:
+    for copy in seeds + token_copies + [meta_copy]:
         copy.start()
     quarter(y)
     quarter(twin)
@@ -277,16 +278,16 @@
         part[who, :, 640:768] = jnp.dot(value, wv[...], preferred_element_type=F32)
 
     own_rows(0, normed[y])
-    for copy in seeds[1:]:
-        copy.wait_recv()
-    weights.begin(1)
-    seeds[0].wait_recv()
-    weights.begin(0)
-    weights.near_steps()
+    for number in range(4):
+        seeds[number].wait_recv()
+        (kv_weights, q_weights)[number // 2].begin(number % 2)
+    kv_weights.near_steps()
+    q_weights.near_steps()
     token_copies[0].wait_recv()
     own_rows(1, other[0])
+    kv_weights.arrive(0)
+    kv_weights.arrive(1)
     token_copies[1].wait_recv()
-    weights.arrive(1)
 
     def part_copy(number, who, src, dst):
         device = {"section": after} if who == 0 else {"section": after, "dp": mate}
@@ -298,15 +299,19 @@
     part_copies += [part_copy(2 + who, who, q_out, q_in) for who in range(2)]
     for who in (1, 0):
         value = normed[twin] if who == 0 else other[1]
-        rest = jnp.dot(value, w1[...], preferred_element_type=F32)
-        kv_out[who] = (part[who, :, 512:768] + rest[:, 128:384]).astype(BF16)
+        for number, weight in enumerate((wk_g, wv_g)):
+            rest = jnp.dot(value, weight[...], preferred_element_type=F32)
+            columns = slice(number * 128, (number + 1) * 128)
+            kv_out[who, :, columns] = (part[who, :, 512 + number * 128:640 + number * 128] + rest).astype(BF16)
         part_copies[who].start()
-        q_out[who, :, 384:512] = (part[who, :, 384:512] + rest[:, 0:128]).astype(BF16)
-    weights.arrive(0)
+    q_weights.arrive(0)
+    q_weights.arrive(1)
     for who in (1, 0):
         value = normed[twin] if who == 0 else other[1]
-        rest = jnp.dot(value, w0[...], preferred_element_type=F32)
-        q_out[who, :, 0:384] = (part[who, :, 0:384] + rest).astype(BF16)
+        for number, weight in enumerate((wq0_g, wq1_g)):
+            rest = jnp.dot(value, weight[...], preferred_element_type=F32)
+            columns = slice(number * 256, (number + 1) * 256)
+            q_out[who, :, columns] = (part[who, :, columns] + rest).astype(BF16)
         part_copies[2 + who].start()
 
     meta_copy.wait_recv()
@@ -354,6 +359,10 @@
         buffer[slot, 128:256] = both[:, 128:256].astype(BF16)
     kvs.begin(0)
     kvs.begin(1)
+    kv_weights.finish()
+    q_weights.finish()
+    for copy in seeds + token_copies + [meta_copy]:
+        copy.wait_send()
 
     run_max[...] = jnp.full(run_max.shape, FLOOR, F32)
     acc[...] = jnp.zeros_like(acc)
@@ -366,6 +375,8 @@
     kvs.near_step(4)
     for copy in part_copies[2:]:
         copy.wait_recv()
+    for copy in part_copies:
+        copy.wait_send()
     for half in range(2):
         rows = slice(half * BLOCK, (half + 1) * BLOCK)
         for head in range(4):
@@ -387,7 +398,11 @@
                5: [(3, 2)], 6: [(3, 3)], 7: [(4, 0), (4, 1), (4, 2), (4, 3)]}
         for number, pieces in due.items():
             @pl.when(t == number)
-            def _(pieces=pieces):
+            def _(pieces=pieces, number=number):
+                if number == 6:
+                    kvs.drain((1, 2), near=True)
+                if number == 7:
+                    kvs.drain((3,))
                 for piece in pieces:
                     kvs.arrive(*piece)
 
@@ -438,13 +453,7 @@
         result = acc[head, :, 0:128] / acc[head, :, 128:256]
         out_ref[:, head * HEAD:(head + 1) * HEAD] = result.astype(BF16)
 
-    for copy in seeds:
-        copy.wait_send()
-    meta_copy.wait_send()
-    for copy in token_copies + part_copies:
-        copy.wait_send()
-    weights.finish()
-    kvs.finish()
+    kvs.drain((4,))
 
 
 def local(tokens, norm_gain, query_weight, key_weight, value_weight, block_order, doc_ids):
@@ -470,8 +479,10 @@
             pltpu.VMEM((deep, 512), BF16),
             pltpu.VMEM((deep, 128), BF16),
             pltpu.VMEM((deep, 128), BF16),
-            pltpu.VMEM((deep, 384), BF16),
-            pltpu.VMEM((deep, 384), BF16),
+            pltpu.VMEM((deep, 128), BF16),
+            pltpu.VMEM((deep, 128), BF16),
+            pltpu.VMEM((deep, 256), BF16),
+            pltpu.VMEM((deep, 256), BF16),
             pltpu.VMEM((2, 128, 768), F32),
             pltpu.VMEM((2, 128, 256), BF16),
             pltpu.VMEM((2, 128, 512), BF16),
@@ -490,6 +501,7 @@
             pltpu.VMEM((128, 1024), F32),
             dma((9,)), dma((2,)), dma((4,)), dma((4,)), dma((2,)), dma((2,)), dma((4,)), dma((4,)),
             dma((2, 4)), dma((2, 4)), dma((2, 3, 4)), dma((2, 3, 4)),
+            dma((2, 4)), dma((2, 4)), dma((2, 3, 4)), dma((2, 3, 4)),
             dma((2, 2, 4)), dma((2, 2, 4)), dma((2, 2, 4, 4)), dma((2, 2, 4, 4)),
         ],
         compiler_params=pltpu.CompilerParams(

time: 83 us -> 79.4 us (0.957)
  the two profiles are of different devices: /device:TPU:114 before, /device:TPU:54 now
where the time goes in v3:
time: 79.4 us; the launch traced here: 79.2 us
  Pallas kernels  77.6 us (98%)
  local copies, waits for them, and re-layouts  1.57 us (2%)
    pallas_call x1, Pallas kernels, local(): pl.pallas_call(kernel, out_shape=jax.ShapeDtypeStruct((128, 512), BF16),...  77.6 us

profile of v3, /device:TPU:54, one launch (start us, length us, event | category | flops | bytes accessed | tf_op | source)
XLA Modules:
  0.0 79.2 jit_solution(8291480553627524479)
XLA Ops:
  0.0 77.6 %relay_attention.1 = bf16[128,512]{1,0:T(8,128)(2,1)} custom-call(bf16[1,1,128,4096]{3,2,1,0:T(8,128)(2,1)} %tok_hbm.1, f32[1,4096]{1,0:T(1,128)} %gain_hbm.1, bf16[1,1024,512]{2,1,0:T(8,128)(2,1)} %wq_hbm.1, bf16[1,1024,128]{2,1,0:T(8,128)(2,1)} %wk_hbm.1, bf16[1,1024,128]{2,1,0:T(8,128)(2,1)} %wv_hbm.1, s32[1,1,128]{2,1,0:T(1,128)} %order_hbm.1, ...), custom_call_target="tpu_custom_call" | custom-call | tf_op jit(solution)/shard_map/relay_attention/pallas_call | solution.py:466
  77.6 1.6 %copy.10 = bf16[1,1,128,512]{3,2,1,0:T(8,128)(2,1)} copy(bf16[1,1,128,512]{3,2,1,0:T(8,128)(2,1)} %bitcast.1) | data formatting | bytes 262144

commit v4 on v3

--- a/solution.py
+++ b/solution.py
@@ -189,8 +189,8 @@
     small_loads = [
         pltpu.make_async_copy(order_hbm.at[0], order_ref, load_sem.at[5]),
         pltpu.make_async_copy(doc_hbm.at[0], doc_ref, load_sem.at[6]),
+        pltpu.make_async_copy(table_hbm, table_ref, load_sem.at[8]),
         pltpu.make_async_copy(gain_hbm, gain_ref, load_sem.at[7]),
-        pltpu.make_async_copy(table_hbm, table_ref, load_sem.at[8]),
     ]
     loads = [
         pltpu.make_async_copy(tok_hbm.at[0, 0], tok, load_sem.at[0]),
@@ -198,7 +198,7 @@
         pltpu.make_async_copy(wk_hbm.at[0], wk, load_sem.at[2]),
         pltpu.make_async_copy(wv_hbm.at[0], wv, load_sem.at[3]),
     ]
-    for load in loads[:1] + small_loads + loads[1:]:
+    for load in loads[:1] + small_loads[::-1] + loads[1:]:
         load.start()
 
     kv_weights = Spread((wk_g, wv_g), x, z, w_ns, w_nr, w_fs, w_fr)
@@ -227,6 +227,35 @@
         seed(2, wq_hbm.at[0, rows0, pl.ds(0, 256)], wq0_g.at[rows0, :]),
         seed(3, wq_hbm.at[0, rows1, pl.ds(256, 256)], wq1_g.at[rows1, :]),
     ]
+
+    loads[0].wait()
+    small_loads[3].wait()
+    wide = tok.shape[1] // 4
+    square = jnp.zeros((128, 128), F32)
+    for column in range(0, tok.shape[1], 128):
+        piece = tok[:, column:column + 128].astype(F32)
+        square = square + piece * piece
+    mean = jnp.sum(square, axis=1, keepdims=True) * (1.0 / tok.shape[1])
+    scale = lax.rsqrt(mean + EPSILON)
+
+    def quarter(number):
+        columns = pl.ds(pl.multiple_of(number * wide, wide), wide)
+        value = tok[:, columns].astype(F32) * scale * gain_ref[:, columns]
+        normed[number] = value.astype(BF16)
+
+    def token_copy(slot, number):
+        return pltpu.make_async_remote_copy(
+            src_ref=normed.at[number], dst_ref=other.at[slot], send_sem=tok_send.at[slot],
+            recv_sem=tok_recv.at[slot], device_id={"dp": mate}, device_id_type=MESH)
+
+    token_copies = [token_copy(0, mate), token_copy(1, 3 - y)]
+    quarter(mate)
+
+    pl.semaphore_wait(barrier, len(greeted))
+    for copy in seeds + token_copies[:1]:
+        copy.start()
+    quarter(3 - y)
+    token_copies[1].start()
 
     meta_out[...] = jnp.zeros_like(meta_out)
     small_loads[0].wait()
@@ -239,34 +268,8 @@
     meta_copy = pltpu.make_async_remote_copy(
         src_ref=meta_out, dst_ref=meta_in, send_sem=meta_sem.at[0], recv_sem=meta_sem.at[1],
         device_id={"section": after}, device_id_type=MESH)
-
-    loads[0].wait()
-    small_loads[2].wait()
-    wide = tok.shape[1] // 4
-    square = jnp.zeros((128, 128), F32)
-    for column in range(0, tok.shape[1], 128):
-        piece = tok[:, column:column + 128].astype(F32)
-        square = square + piece * piece
-    mean = jnp.sum(square, axis=1, keepdims=True) * (1.0 / tok.shape[1])
-    scale = lax.rsqrt(mean + EPSILON)
-
-    def quarter(number):
-        columns = pl.ds(pl.multiple_of(number * wide, wide), wide)
-        value = tok[:, columns].astype(F32) * scale * gain_ref[:, columns]
-        normed[number] = value.astype(BF16)
-
-    def token_copy(slot, number):
-        return pltpu.make_async_remote_copy(
-            src_ref=normed.at[number], dst_ref=other.at[slot], send_sem=tok_send.at[slot],
-            recv_sem=tok_recv.at[slot], device_id={"dp": mate}, device_id_type=MESH)
-
-    token_copies = [token_copy(0, mate), token_copy(1, 3 - y)]
-    quarter(mate)
-    quarter(3 - y)
-
-    pl.semaphore_wait(barrier, len(greeted))
-    for copy in seeds + token_copies + [meta_copy]:
-        copy.start()
+    meta_copy.start()
+
     quarter(y)
     quarter(twin)
     for load in loads[1:]:
@@ -287,7 +290,6 @@
     own_rows(1, other[0])
     kv_weights.arrive(0)
     kv_weights.arrive(1)
-    token_copies[1].wait_recv()
 
     def part_copy(number, who, src, dst):
         device = {"section": after} if who == 0 else {"section": after, "dp": mate}
@@ -297,7 +299,9 @@
 
     part_copies = [part_copy(who, who, kv_out, kv_in) for who in range(2)]
     part_copies += [part_copy(2 + who, who, q_out, q_in) for who in range(2)]
-    for who in (1, 0):
+    for who in (0, 1):
+        if who == 1:
+            token_copies[1].wait_recv()
         value = normed[twin] if who == 0 else other[1]
         for number, weight in enumerate((wk_g, wv_g)):
             rest = jnp.dot(value, weight[...], preferred_element_type=F32)
@@ -315,7 +319,7 @@
         part_copies[2 + who].start()
 
     meta_copy.wait_recv()
-    small_loads[3].wait()
+    small_loads[2].wait()
     to_scalars = pltpu.make_async_copy(meta_in, meta_s, load_sem.at[4])
     to_scalars.start()
     to_scalars.wait()
@@ -357,8 +361,7 @@
         buffer = kv0 if half == 0 else kv1
         buffer[slot, 0:128] = turned(both[:, 0:128], half).astype(BF16)
         buffer[slot, 128:256] = both[:, 128:256].astype(BF16)
-    kvs.begin(0)
-    kvs.begin(1)
+        kvs.begin(half)
     kv_weights.finish()
     q_weights.finish()
     for copy in seeds + token_copies + [meta_copy]:

time: 79.4 us -> 79.4 us (level)
  the two profiles are of different devices: /device:TPU:54 before, /device:TPU:20 now
where the time goes in v4:
time: 79.4 us; the launch traced here: 79.2 us
  Pallas kernels  77.7 us (98%)
  local copies, waits for them, and re-layouts  1.57 us (2%)
    pallas_call x1, Pallas kernels, local(): pl.pallas_call(kernel, out_shape=jax.ShapeDtypeStruct((128, 512), BF16),...  77.7 us

profile of v4, /device:TPU:20, one launch (start us, length us, event | category | flops | bytes accessed | tf_op | source)
XLA Modules:
  0.0 79.2 jit_solution(13150414805912833525)
XLA Ops:
  0.0 77.7 %relay_attention.1 = bf16[128,512]{1,0:T(8,128)(2,1)} custom-call(bf16[1,1,128,4096]{3,2,1,0:T(8,128)(2,1)} %tok_hbm.1, f32[1,4096]{1,0:T(1,128)} %gain_hbm.1, bf16[1,1024,512]{2,1,0:T(8,128)(2,1)} %wq_hbm.1, bf16[1,1024,128]{2,1,0:T(8,128)(2,1)} %wk_hbm.1, bf16[1,1024,128]{2,1,0:T(8,128)(2,1)} %wv_hbm.1, s32[1,1,128]{2,1,0:T(1,128)} %order_hbm.1, ...), custom_call_target="tpu_custom_call" | custom-call | tf_op jit(solution)/shard_map/relay_attention/pallas_call | solution.py:469
  77.7 1.6 %copy.10 = bf16[1,1,128,512]{3,2,1,0:T(8,128)(2,1)} copy(bf16[1,1,128,512]{3,2,1,0:T(8,128)(2,1)} %bitcast.1) | data formatting | bytes 262144
